TPU v7x, 32 devices: a whole 2x2x4 slice. The times are simulated.
32 devices in a mesh: sec: 4 (over y, x), mpo: 8 (over z, core).
Axes of the slice: x: 2, y: 2, z: 4, core: 2. Of those that a mesh axis runs over, the one named last changes fastest.
Arguments:
- wavefunction: bfloat16 [64, 128, 128], P('sec')
- left_size: int32 [64], P('sec'), may hold values from 32 to 128, as said below
- right_size: int32 [64], replicated, may hold values from 32 to 128, as said below
- right_sector: int32 [64], replicated, may hold values from 0 to 63, as said below
- left_environment: bfloat16 [16, 64, 128, 128], P('mpo', 'sec')
- right_environment: bfloat16 [16, 64, 128, 128], P('mpo', 'sec')
- term_weights: float32 [16], P('mpo'), may hold values from -0.4 to 0.4
Outputs:
- next_vector: float32 [64, 128, 128], P('sec', 'mpo')
- residual: float32 [64, 128, 128], P('sec', 'mpo')
- coefficients: float32 [3], replicated
Inputs may be any that keep to these rules, and one draw needn't show every extreme that they name: `left_size`: some left sector has all 128 rows live. `right_size`: some right sector has all 128 columns live. `right_sector`: a permutation of the 64 sectors; of the left sectors of one index of sec (16 in a row) at most 6 pair with right sectors of any one index of sec (also 16 in a row), and some such pair of indices has exactly 6.
All inputs are finite; a program needn't handle non-finite values.
Results may differ from a plain program's by a relative error of at most 0.0064.
Values may be sent and summed in bfloat16 or wider, within the bound.
A program may use at most 64 MiB of HBM per device.

v0:
```python
import jax
import jax.numpy as jnp
from jax import lax
from jax.sharding import PartitionSpec as P


def route_matches(right_sector, blocks, devices, capacity):
    owners = (right_sector // blocks).reshape(devices, blocks)
    targets = jnp.arange(devices, dtype=jnp.int32)
    onehot = (owners[:, :, None] == targets[None, None, :]).astype(jnp.int32)
    earlier = jnp.cumsum(onehot, axis=1) - onehot
    position = jnp.sum(earlier * onehot, axis=2)
    places = owners * capacity + position
    slot_ids = jnp.arange(devices * capacity, dtype=jnp.int32)
    matches = (places[:, :, None] == slot_ids[None, None, :]).astype(jnp.int32)
    return (places, matches)


def shards(
    wavefunction,
    left_size,
    right_size,
    right_sector,
    left_environment,
    right_environment,
    term_weights,
):
    blocks = wavefunction.shape[0]
    width = wavefunction.shape[1]
    terms = left_environment.shape[0]
    devices = lax.axis_size("sec")
    layers = lax.axis_size("mpo")
    average = blocks // devices
    capacity = average + max(1, average // 2)
    sec_index = lax.axis_index("sec")
    mpo_index = lax.axis_index("mpo")
    entries = float(blocks * devices * width * width)
    places, matches = route_matches(right_sector, blocks, devices, capacity)
    own_places = lax.dynamic_index_in_dim(places, sec_index, 0, keepdims=False)
    own_matches = lax.dynamic_index_in_dim(matches, sec_index, 0, keepdims=False)
    block_ids = jnp.arange(blocks, dtype=jnp.int32)
    send_source = jnp.sum(block_ids[:, None] * own_matches, axis=0)
    send_valid = jnp.sum(own_matches, axis=0) > 0
    incoming = lax.dynamic_slice_in_dim(matches, sec_index * capacity, capacity, 2)
    sector_grid = right_sector.reshape(devices, blocks)
    arrived_valid = jnp.sum(incoming, axis=1) > 0
    arrived_sector = jnp.sum(sector_grid[:, :, None] * incoming, axis=1)
    arrived_local = jnp.where(arrived_valid, arrived_sector - sec_index * blocks, 0).reshape(-1)
    own_sector = lax.dynamic_slice_in_dim(right_sector, sec_index * blocks, blocks, 0)
    positions = jnp.arange(width, dtype=jnp.int32)
    partner_size = jnp.take(right_size, own_sector, axis=0)
    row_live = (positions[None, :] < left_size[:, None]).astype(jnp.float32)
    col_live = (positions[None, :] < partner_size[:, None]).astype(jnp.float32)
    live_mask = row_live[:, :, None] * col_live[:, None, :]

    def apply_operator(vector):
        rounded = vector.astype(jnp.bfloat16)
        half_term = jnp.einsum(
            "wsab,sbc->swac", left_environment, rounded, preferred_element_type=jnp.float32
        )
        half_term = (term_weights[None, :, None, None] * half_term).astype(jnp.bfloat16)
        outgoing = jnp.where(
            send_valid[:, None, None, None],
            jnp.take(half_term, send_source, axis=0),
            jnp.zeros((), jnp.bfloat16),
        )
        outgoing = outgoing.reshape(devices, capacity, terms, width, width)
        arrived = lax.all_to_all(outgoing, "sec", split_axis=0, concat_axis=0, tiled=True)
        arrived = arrived.reshape(devices * capacity, terms, width, width)
        right_terms = jnp.take(right_environment, arrived_local, axis=1)
        partial_value = jnp.einsum(
            "kwac,wkdc->kad", arrived, right_terms, preferred_element_type=jnp.float32
        )
        partial_value = partial_value.reshape(devices, capacity, width, width)
        summed = lax.psum(partial_value, "mpo")
        returned = lax.all_to_all(summed, "sec", split_axis=0, concat_axis=0, tiled=True)
        applied = jnp.take(returned.reshape(devices * capacity, width, width), own_places, axis=0)
        return live_mask * applied

    def rayleigh(basis_vec, applied_vec):
        return lax.psum(jnp.sum(basis_vec * applied_vec), "sec")

    masked_start = live_mask * wavefunction.astype(jnp.float32)
    start_total = lax.psum(jnp.sum(masked_start * masked_start), "sec")
    first_vector = masked_start / jnp.sqrt(start_total / entries + 1e-06)
    image_first = apply_operator(first_vector)
    alpha_first = rayleigh(first_vector, image_first) / entries
    lanczos_rest = image_first - alpha_first * first_vector
    rest_total = lax.psum(jnp.sum(lanczos_rest * lanczos_rest), "sec")
    beta_next = jnp.sqrt(rest_total / entries + 1e-06)
    next_vector = lanczos_rest / beta_next
    image_next = apply_operator(next_vector)
    alpha_next = rayleigh(next_vector, image_next) / entries
    residual = image_next - alpha_next * next_vector - beta_next * first_vector
    row_count = width // layers
    next_slice = lax.dynamic_slice_in_dim(next_vector, mpo_index * row_count, row_count, 1)
    residual_slice = lax.dynamic_slice_in_dim(residual, mpo_index * row_count, row_count, 1)
    coefficients = jnp.stack([alpha_first, beta_next, alpha_next])
    return (next_slice, residual_slice, coefficients)


def solution(mesh):
    placed = (
        P("sec", None, None),
        P("sec"),
        P(),
        P(),
        P("mpo", "sec", None, None),
        P("mpo", "sec", None, None),
        P("mpo"),
    )
    return jax.shard_map(
        shards,
        mesh=mesh,
        in_specs=placed,
        out_specs=(P("sec", "mpo", None), P("sec", "mpo", None), P()),
        check_vma=False,
    )
```

profile of v0, /device:TPU:0, one launch (start us, length us, event | category | flops | bytes accessed | tf_op | source)
XLA Modules:
  0.0 299.7 jit_solution(8701571508518069777)
XLA Ops:
  12.8 2.0 multiply_reduce_fusion.3
  14.7 12.0 %psum.42 = f32[]{:T(128)} all-reduce(f32[]{:T(128)} %multiply_reduce_fusion.3), channel_id=1, replica_groups=mesh['sec'=4,'mpo'=8] {'sec'}, use_global_device_ids=true, to_apply=%region_4.5 | all-reduce | flops 1 | bytes 8 | tf_op jit(solution)/shard_map/psum | solution.py:84
  27.9 2.9 fusion.4
  30.8 2.1 gather_fusion.1
  34.3 4.3 %all-to-all-start = ((bf16[4,6,2,128,128]{3,4,2,1,0:T(8,128)(2,1)}), bf16[4,6,2,128,128]{3,4,2,1,0:T(8,128)(2,1)}, u32[]{:S(2)}, u32[]{:S(2)}) async-start(bf16[4,6,2,128,128]{3,4,2,1,0:T(8,128)(2,1)} %bitcast.4), calls=%async_computation | async-start | bytes 3145728 | tf_op jit(solution)/shard_map/all_to_all | solution.py:68
  38.7 2.1 gather_fusion.2
  40.8 15.4 %all-to-all-done = bf16[4,6,2,128,128]{3,4,2,1,0:T(8,128)(2,1)} async-done(((bf16[4,6,2,128,128]{3,4,2,1,0:T(8,128)(2,1)}), bf16[4,6,2,128,128]{3,4,2,1,0:T(8,128)(2,1)}, u32[]{:S(2)}, u32[]{:S(2)}) %all-to-all-start) | async-done | bytes 1572896 | tf_op jit(solution)/shard_map/all_to_all | solution.py:68
  56.2 3.2 %fusion.2 = f32[24,128,128,1]{2,1,3,0:T(8,128)} fusion(bf16[24,2,128,128]{2,3,1,0:T(8,128)(2,1)} %bitcast.28, bf16[24,2,128,128]{3,2,1,0:T(8,128)(2,1)S(1)} %gather_fusion.2, pred[24]{0:T(512)(128)(4,1)S(1)} %compare_and_fusion.1), kind=kOutput, calls=%fused_computation.13 | convolution fusion | flops 202113024 | bytes 4718616 | tf_op jit(solution)/shard_map/kwac,wkdc->kad/dot_general | solution.py:71
  59.5 62.5 %all-reduce.3.cloned.1.call-done = f32[4,6,128,128]{3,2,1,0:T(8,128)} async-done(((f32[4,6,128,128]{3,2,1,0:T(8,128)}), f32[4,6,128,128]{3,2,1,0:T(8,128)}) %all-reduce.3.cloned.1.call-update) | async-done | bytes 1572880 | tf_op jit(solution)/shard_map/psum | solution.py:75
  122.0 3.6 %all-to-all-start.1 = ((f32[4,6,128,128]{3,2,1,0:T(8,128)}), f32[4,6,128,128]{3,2,1,0:T(8,128)S(1)}, u32[]{:S(2)}, u32[]{:S(2)}) async-start(f32[4,6,128,128]{3,2,1,0:T(8,128)} %all-reduce.3.cloned.1.call-done), calls=%async_computation.1 | async-start | bytes 3145728 | tf_op jit(solution)/shard_map/all_to_all | solution.py:76
  125.7 17.4 %all-to-all-done.1 = f32[4,6,128,128]{3,2,1,0:T(8,128)S(1)} async-done(((f32[4,6,128,128]{3,2,1,0:T(8,128)}), f32[4,6,128,128]{3,2,1,0:T(8,128)S(1)}, u32[]{:S(2)}, u32[]{:S(2)}) %all-to-all-start.1) | async-done | bytes 1572896 | tf_op jit(solution)/shard_map/all_to_all | solution.py:76
  144.2 2.0 gather_fusion.3
  147.2 9.5 %psum.44 = f32[]{:T(128)} all-reduce(f32[]{:T(128)} %multiply_reduce_fusion.2), channel_id=1, replica_groups=mesh['sec'=4,'mpo'=8] {'sec'}, use_global_device_ids=true, to_apply=%region_10.14 | all-reduce | flops 1 | bytes 8 | tf_op jit(solution)/shard_map/psum | solution.py:81
  158.4 9.5 %psum.45 = f32[]{:T(128)} all-reduce(f32[]{:T(128)} %multiply_reduce_fusion.1), channel_id=1, replica_groups=mesh['sec'=4,'mpo'=8] {'sec'}, use_global_device_ids=true, to_apply=%region_12.16 | all-reduce | flops 1 | bytes 8 | tf_op jit(solution)/shard_map/psum | solution.py:89
  168.6 2.5 broadcast_divide_fusion
  171.6 1.9 gather_fusion.4
  175.3 16.9 %all_to_all.20 = bf16[4,6,2,128,128]{3,4,2,1,0:T(8,128)(2,1)S(1)} all-to-all(bf16[4,6,2,128,128]{3,4,2,1,0:T(8,128)(2,1)S(1)} %bitcast.51), channel_id=1, replica_groups=mesh['sec'=4,'mpo'=8] {'sec'}, dimensions={0} | all-to-all | bytes 3145728 | tf_op jit(solution)/shard_map/all_to_all | solution.py:68
  192.2 1.8 fusion
  194.0 60.5 %all-reduce.5.cloned.1.call-done = f32[4,6,128,128]{3,2,1,0:T(8,128)} async-done(((f32[4,6,128,128]{3,2,1,0:T(8,128)}), f32[4,6,128,128]{3,2,1,0:T(8,128)}) %all-reduce.5.cloned.1.call-update) | async-done | bytes 1572880 | tf_op jit(solution)/shard_map/psum | solution.py:75
  254.5 4.3 %all-to-all-start.3 = ((f32[4,6,128,128]{3,2,1,0:T(8,128)}), f32[4,6,128,128]{3,2,1,0:T(8,128)}, u32[]{:S(2)}, u32[]{:S(2)}) async-start(f32[4,6,128,128]{3,2,1,0:T(8,128)} %all-reduce.5.cloned.1.call-done), calls=%async_computation.3 | async-start | bytes 3145728 | tf_op jit(solution)/shard_map/all_to_all | solution.py:76
  258.9 17.6 %all-to-all-done.3 = f32[4,6,128,128]{3,2,1,0:T(8,128)} async-done(((f32[4,6,128,128]{3,2,1,0:T(8,128)}), f32[4,6,128,128]{3,2,1,0:T(8,128)}, u32[]{:S(2)}, u32[]{:S(2)}) %all-to-all-start.3) | async-done | bytes 1572896 | tf_op jit(solution)/shard_map/all_to_all | solution.py:76
  276.4 2.0 gather_fusion.5
  278.5 2.0 multiply_reduce_fusion
  280.4 9.5 %psum.47 = f32[]{:T(128)} all-reduce(f32[]{:T(128)} %get-tuple-element.10), channel_id=1, replica_groups=mesh['sec'=4,'mpo'=8] {'sec'}, use_global_device_ids=true, to_apply=%region_15.19 | all-reduce | flops 1 | bytes 8 | tf_op jit(solution)/shard_map/psum | solution.py:81
  (51 shorter events, 15.3 us)
Async XLA Ops:
  7.2 20.8 %copy-start = (bf16[2,16,128,128]{3,2,1,0:T(8,128)(2,1)S(1)}, bf16[2,16,128,128]{3,2,1,0:T(8,128)(2,1)}, u32[]{:S(2)}) copy-start(bf16[2,16,128,128]{3,2,1,0:T(8,128)(2,1)} %param.17) | copy-start | bytes 3145732
  34.3 21.9 %all-to-all-start = ((bf16[4,6,2,128,128]{3,4,2,1,0:T(8,128)(2,1)}), bf16[4,6,2,128,128]{3,4,2,1,0:T(8,128)(2,1)}, u32[]{:S(2)}, u32[]{:S(2)}) async-start(bf16[4,6,2,128,128]{3,4,2,1,0:T(8,128)(2,1)} %bitcast.4), calls=%async_computation | async-start | bytes 3145728 | tf_op jit(solution)/shard_map/all_to_all | solution.py:68
  38.7 83.3 %all-reduce.3.cloned.1.call-start = ((), (), s32[]{:S(2)}) async-start(), calls=%async_computation.4 | async-start | bytes 3145728 | tf_op jit(solution)/shard_map/psum | solution.py:75
  40.8 18.6 %copy-start.1 = (bf16[24,2,128,128]{3,2,1,0:T(8,128)(2,1)}, bf16[24,2,128,128]{3,2,1,0:T(8,128)(2,1)S(1)}, u32[]{:S(2)}) copy-start(bf16[24,2,128,128]{3,2,1,0:T(8,128)(2,1)S(1)} %gather_fusion.2) | copy-start | bytes 4718596
  122.0 21.0 %all-to-all-start.1 = ((f32[4,6,128,128]{3,2,1,0:T(8,128)}), f32[4,6,128,128]{3,2,1,0:T(8,128)S(1)}, u32[]{:S(2)}, u32[]{:S(2)}) async-start(f32[4,6,128,128]{3,2,1,0:T(8,128)} %all-reduce.3.cloned.1.call-done), calls=%async_computation.1 | async-start | bytes 3145728 | tf_op jit(solution)/shard_map/all_to_all | solution.py:76
  125.6 20.7 %copy-start.3 = (bf16[16,128,128]{2,1,0:T(8,128)(2,1)S(1)}, bf16[16,128,128]{2,1,0:T(8,128)(2,1)}, u32[]{:S(2)}) copy-start(bf16[16,128,128]{2,1,0:T(8,128)(2,1)} %param.13) | copy-start | bytes 1572868
  125.6 128.9 %all-reduce.5.cloned.1.call-start = ((), (), s32[]{:S(2)}) async-start(), calls=%async_computation.5 | async-start | bytes 3145728 | tf_op jit(solution)/shard_map/psum | solution.py:75
  143.1 1.1 copy-start.4
  168.6 2.5 copy-start.5
  175.3 16.9 %copy-start.2 = (bf16[24,2,128,128]{3,2,1,0:T(8,128)(2,1)S(1)}, bf16[24,2,128,128]{3,2,1,0:T(8,128)(2,1)}, u32[]{:S(2)}) copy-start(bf16[24,2,128,128]{3,2,1,0:T(8,128)(2,1)} %copy-done.1) | copy-start | bytes 4718596
  254.5 21.9 %all-to-all-start.3 = ((f32[4,6,128,128]{3,2,1,0:T(8,128)}), f32[4,6,128,128]{3,2,1,0:T(8,128)}, u32[]{:S(2)}, u32[]{:S(2)}) async-start(f32[4,6,128,128]{3,2,1,0:T(8,128)} %all-reduce.5.cloned.1.call-done), calls=%async_computation.3 | async-start | bytes 3145728 | tf_op jit(solution)/shard_map/all_to_all | solution.py:76
Sparse Core Ops, SparseCore 0:
  59.6 62.3 all-reduce.2
  194.1 60.3 all-reduce.4
where the time goes:
time: 301 us; the launch traced here: 300 us
  waiting for transfers between devices  173 us (57%)
  blocking collectives  57.4 us (19%)
  other arithmetic  17.4 us (6%)
  between operations  16.9 us (6%)
  local copies, waits for them, and re-layouts  13.8 us (5%)
  starting transfers between devices  12.3 us (4%)
  matrix products  8.4 us (3%)
    psum x2, waiting for transfers between devices, apply_operator(): summed = lax.psum(partial_value, 'mpo')  123 us
    all_to_all x2, waiting for transfers between devices, apply_operator(): lax.all_to_all(summed, 'sec', split_axis=0, concat_axis=0, tiled=True)  34.9 us
    psum x2, blocking collectives, rayleigh(): return lax.psum(jnp.sum(basis_vec * applied_vec), 'sec')  19 us
    all_to_all x1, blocking collectives, apply_operator(): lax.all_to_all(outgoing, 'sec', split_axis=0, concat_axis=0, tiled=True)  16.9 us
    all_to_all x1, waiting for transfers between devices, apply_operator(): lax.all_to_all(outgoing, 'sec', split_axis=0, concat_axis=0, tiled=True)  15.4 us
    psum x1, blocking collectives, shards(): start_total = lax.psum(jnp.sum(masked_start * masked_start), 'sec')  12 us
    psum x1, blocking collectives, shards(): rest_total = lax.psum(jnp.sum(lanczos_rest * lanczos_rest), 'sec')  9.53 us
    all_to_all x2, starting transfers between devices, apply_operator(): lax.all_to_all(summed, 'sec', split_axis=0, concat_axis=0, tiled=True)  7.9 us
  transfers between devices with their start and end apart: 5, of which 5 were waited for; matrix products, arithmetic and copies ran while one was open for 1% of the time, Pallas kernels for 0%

commit v1 on v0

v1 whole, which is shorter than its diff:
```python
import functools

import jax
import jax.numpy as jnp
from jax import lax
from jax.experimental import pallas as pl
from jax.experimental.pallas import tpu as pltpu
from jax.sharding import PartitionSpec as P

F32 = jnp.float32
BF16 = jnp.bfloat16
GROUPS = 2
UNROLL = 4


def flip(index, mask, size):
    out = index
    bit = 1
    while bit < size:
        if mask & bit:
            out = out + bit * (1 - 2 * ((index // bit) % 2))
        bit *= 2
    return out


def tree(values):
    values = list(values)
    while len(values) > 1:
        values = [values[i] + values[i + 1] for i in range(0, len(values), 2)]
    return values[0]


def fold(x):
    return jnp.sum(x.reshape(-1, 8, x.shape[-1]), axis=0)


def total(tile):
    return jnp.sum(jnp.sum(tile, axis=1, keepdims=True), axis=0, keepdims=True)


def kernel(
    devices, layers, capacity,
    wave, left_size, right_size, right_sector, left_env, right_env, weights,
    next_out, rest_out, coef_out,
    staged, held, place, first, half, mask, part, pair_in, z_out, z_in, gathered,
    norm_tiles, layer_tiles, sec_tiles, layer_tile2, sec_tile2,
    env_send, env_recv, local_sem, norm_send, norm_recv,
    pair_send, pair_recv, z_send, z_recv,
    gather_send, gather_recv, relay_send, relay_recv,
    layer_send, layer_recv, sec_send, sec_recv,
):
    blocks, width = wave.shape[0], wave.shape[1]
    terms = left_env.shape[0]
    depth = layers // 2
    rows = width // layers
    per_group = blocks // GROUPS
    entries = float(blocks * devices * width * width)
    sec = lax.axis_index("sec")
    mpo = lax.axis_index("mpo")
    z, core = mpo // 2, mpo % 2
    partner = 2 * z + 1 - core
    sec_peer = [flip(sec, k, devices) for k in range(devices)]
    mpo_peer = [flip(mpo, k, layers) for k in range(layers)]
    z_peer = [flip(z, k, depth) for k in range(depth)]
    order = list(range(depth - 1, 0, -1))
    started = []

    def send(src, dst, send_sem, recv_sem, to):
        copy = pltpu.make_async_remote_copy(
            src_ref=src, dst_ref=dst, send_sem=send_sem, recv_sem=recv_sem,
            device_id=to, device_id_type=pl.DeviceIdType.MESH,
        )
        copy.start()
        started.append(copy)
        return copy

    barrier = pltpu.get_barrier_semaphore()
    for k in range(1, devices):
        pl.semaphore_signal(barrier, inc=1, device_id=(sec_peer[k], mpo), device_id_type=pl.DeviceIdType.MESH)
    for k in range(1, layers):
        pl.semaphore_signal(barrier, inc=1, device_id=(sec, mpo_peer[k]), device_id_type=pl.DeviceIdType.MESH)

    own_start = (devices - 1) * capacity
    locals_ = []
    for t in range(terms):
        copy = pltpu.make_async_copy(right_env.at[t], held.at[t, pl.ds(own_start, blocks)], local_sem.at[t])
        copy.start()
        locals_.append(copy)

    def pack(k):
        base = sec_peer[k] * blocks

        def look(i, carry):
            count, found = carry[0], carry[1:]
            local = right_sector[base + i] - sec * blocks
            mine = (local >= 0) & (local < blocks)
            found = tuple(
                jnp.where(mine & (count == c), local, found[c]) for c in range(capacity)
            )
            return (count + mine.astype(jnp.int32),) + found

        carry = (jnp.int32(0),) * (capacity + 1)
        for i in range(blocks):
            carry = look(i, carry)
        for c in range(capacity):
            for t in range(terms):
                staged[k - 1, t, c] = right_env[t, carry[1 + c]]

    env_copies = []
    peer_order = list(range(devices - 1, 0, -1))
    for n, k in enumerate(peer_order):
        pack(k)
        if n == 0:
            pl.semaphore_wait(barrier, devices - 1 + layers - 1)
        for t in range(terms):
            env_copies.append(send(
                staged.at[k - 1, t], held.at[t, pl.ds((k - 1) * capacity, capacity)],
                env_send.at[k - 1, t], env_recv.at[k - 1, t], (sec_peer[k], mpo),
            ))

    counts = [jnp.int32(0)] * devices
    for i in range(blocks):
        sector = right_sector[sec * blocks + i]
        owner = sector // blocks
        at = own_start + sector - sec * blocks
        for k in range(1, devices):
            match = owner == sec_peer[k]
            at = jnp.where(match, (k - 1) * capacity + counts[k], at)
            counts[k] = counts[k] + match.astype(jnp.int32)
        place[i] = at

    row_ids = lax.broadcasted_iota(jnp.int32, (width, width), 0)
    col_ids = lax.broadcasted_iota(jnp.int32, (width, width), 1)
    slice_rows = lax.broadcasted_iota(jnp.int32, (rows, width), 0) + mpo * rows
    slice_cols = lax.broadcasted_iota(jnp.int32, (rows, width), 1)

    def masked_block(l, acc):
        live_rows = left_size[l]
        live_cols = right_size[right_sector[sec * blocks + l]]
        live = (row_ids < live_rows) & (col_ids < live_cols)
        block = jnp.where(live, wave[l].astype(F32), 0.0)
        first[l] = block
        live = (slice_rows < live_rows) & (slice_cols < live_cols)
        mask[l] = jnp.where(live, 1.0, 0.0)
        return acc + fold(block * block)

    norm_tiles[0] = lax.fori_loop(0, blocks, masked_block, jnp.zeros((8, width), F32))
    norm_copies = [
        send(norm_tiles.at[0], norm_tiles.at[k], norm_send.at[k], norm_recv.at[k], (sec_peer[k], mpo))
        for k in range(1, devices)
    ]
    for copy in norm_copies:
        copy.wait_recv()
    start_total = total(tree([norm_tiles[k] for k in range(devices)]))
    scale = 1.0 / jnp.sqrt(start_total * (1.0 / entries) + 1e-6)

    def left_block(l, v):
        stacked = jnp.concatenate([left_env[t, l] for t in range(terms)], axis=0)
        product = jnp.dot(stacked, v, preferred_element_type=F32)
        half[l] = jnp.concatenate(
            [(weights[t] * product[t * width:(t + 1) * width]).astype(BF16) for t in range(terms)], axis=1
        )

    def right_block(h, l):
        at = place[l]
        right = jnp.concatenate([held[t, at] for t in range(terms)], axis=1)
        out = lax.dot_general(half[l], right, (((1,), (1,)), ((), ())), preferred_element_type=F32)
        for m in range(layers):
            part[h, m % 2, m // 2, l] = out[m * rows:(m + 1) * rows]

    def loop_blocks(begin, end, body):
        def several(i, carry):
            for u in range(UNROLL):
                body(begin + i * UNROLL + u)
            return carry
        lax.fori_loop(0, (end - begin) // UNROLL, several, 0)

    def flat(g):
        return pl.ds(g * per_group * rows, per_group * rows)

    def pair_exchange(h, g):
        span = pl.ds(g * per_group, per_group)
        return {
            k: send(
                part.at[h, 1 - core, z_peer[k], span], pair_in.at[h, k, span],
                pair_send.at[h, g, k], pair_recv.at[h, g, k], (sec, partner),
            )
            for k in order + [0]
        }

    def z_exchange(h, g, pair_copies):
        span = pl.ds(g * per_group, per_group)
        copies = []
        for k in order:
            pair_copies[k].wait_recv()
            both = part[h, core, z_peer[k], span] + pair_in[h, k, span]
            z_out[h, k - 1, flat(g)] = both.reshape(per_group * rows, width).astype(BF16)
            copies.append(send(
                z_out.at[h, k - 1, flat(g)], z_in.at[h, k - 1, flat(g)],
                z_send.at[h, g, k - 1], z_recv.at[h, g, k - 1], (sec, 2 * z_peer[k] + core),
            ))
        pair_copies[0].wait_recv()
        return copies

    def image(h, z_copies):
        for copy in z_copies:
            copy.wait_recv()
        value = part[h, core, z] + pair_in[h, 0]
        for k in range(1, depth):
            value = value + z_in[h, k - 1].astype(F32).reshape(blocks, rows, width)
        return mask[...] * value

    def first_left(l):
        left_block(l, (first[l] * scale).astype(BF16))

    loop_blocks(0, blocks, first_left)
    for copy in locals_:
        copy.wait()
    for copy in env_copies:
        copy.wait_recv()
    pairs, z_copies = {}, []
    for g in range(GROUPS):
        loop_blocks(g * per_group, (g + 1) * per_group, functools.partial(right_block, 0))
        pairs[g] = pair_exchange(0, g)
        if g > 0:
            z_copies += z_exchange(0, g - 1, pairs[g - 1])
    z_copies += z_exchange(0, GROUPS - 1, pairs[GROUPS - 1])
    first_slice = first[:, pl.ds(pl.multiple_of(mpo * rows, rows), rows), :] * scale
    image_first = image(0, z_copies)

    inner = fold(first_slice * image_first)
    square = fold(first_slice * first_slice)
    lean = jnp.where(square > 1e-30, inner / jnp.where(square > 1e-30, square, 1.0), 0.0)
    away = image_first - lean[None, :, :] * first_slice if rows == 8 else (
        image_first - jnp.concatenate([lean] * (rows // 8), axis=0)[None] * first_slice
    )
    layer_tiles[0, 0] = inner
    layer_tiles[0, 1] = square
    layer_tiles[0, 2] = fold(away * away)
    layer_tiles[0, 3] = lean
    copies = [
        send(layer_tiles.at[0], layer_tiles.at[k], layer_send.at[0, k], layer_recv.at[0, k], (sec, mpo_peer[k]))
        for k in range(1, layers)
    ]
    for copy in copies:
        copy.wait_recv()

    def moved(a, inner, square, spread, lean):
        d = a - lean
        return spread - 2.0 * d * (inner - lean * square) + d * square * d

    inner = tree([layer_tiles[k, 0] for k in range(layers)])
    square = tree([layer_tiles[k, 1] for k in range(layers)])
    lean = jnp.where(square > 1e-30, inner / jnp.where(square > 1e-30, square, 1.0), 0.0)
    spread = tree([
        moved(lean, layer_tiles[k, 0], layer_tiles[k, 1], layer_tiles[k, 2], layer_tiles[k, 3])
        for k in range(layers)
    ])
    sec_tiles[0, 0] = inner
    sec_tiles[0, 1] = square
    sec_tiles[0, 2] = spread
    sec_tiles[0, 3] = lean
    copies = [
        send(sec_tiles.at[0], sec_tiles.at[k], sec_send.at[0, k], sec_recv.at[0, k], (sec_peer[k], mpo))
        for k in range(1, devices)
    ]
    for copy in copies:
        copy.wait_recv()
    alpha_first = total(tree([sec_tiles[k, 0] for k in range(devices)])) * (1.0 / entries)
    rest_total = total(tree([
        moved(alpha_first, sec_tiles[k, 0], sec_tiles[k, 1], sec_tiles[k, 2], sec_tiles[k, 3])
        for k in range(devices)
    ]))
    beta = jnp.sqrt(rest_total * (1.0 / entries) + 1e-6)
    next_slice = (image_first - alpha_first[None] * first_slice) / beta[None]

    gathered[mpo] = next_slice.reshape(blocks * rows, width).astype(BF16)
    direct, relayed = {}, {}
    for g in range(GROUPS):
        for k in order:
            direct[g, k] = send(
                gathered.at[mpo, flat(g)], gathered.at[mpo, flat(g)],
                gather_send.at[g, k], gather_recv.at[g, k], (sec, 2 * z_peer[k] + core),
            )
        relayed[g, 0] = send(
            gathered.at[mpo, flat(g)], gathered.at[mpo, flat(g)],
            relay_send.at[g, 0], relay_recv.at[g, 0], (sec, partner),
        )
    next_out[...] = next_slice

    def next_block(l):
        if rows % 16 == 0:
            pieces = [gathered[m, pl.ds(pl.multiple_of(l * rows, rows), rows)] for m in range(layers)]
            return jnp.concatenate(pieces, axis=0)
        pieces = [
            gathered[m, pl.ds((l * rows) // 16 * 16, 16)].astype(F32)[(l * rows) % 16:(l * rows) % 16 + rows]
            for m in range(layers)
        ]
        return jnp.concatenate(pieces, axis=0).astype(BF16)

    def second_block(l):
        left_block(l, next_block(l))

    pairs, z_copies = {}, []
    for g in range(GROUPS):
        for k in reversed(order):
            direct[g, k].wait_recv()
            from_there = 2 * z_peer[k] + core
            relayed[g, k] = send(
                gathered.at[from_there, flat(g)], gathered.at[from_there, flat(g)],
                relay_send.at[g, k], relay_recv.at[g, k], (sec, partner),
            )
        for k in [0] + order[::-1]:
            relayed[g, k].wait_recv()
        begin, end = g * per_group, (g + 1) * per_group
        if rows % 16 == 0:
            loop_blocks(begin, end, second_block)
        else:
            for l in range(begin, end):
                second_block(l)
        loop_blocks(begin, end, functools.partial(right_block, 1))
        pairs[g] = pair_exchange(1, g)
        if g > 0:
            z_copies += z_exchange(1, g - 1, pairs[g - 1])
    z_copies += z_exchange(1, GROUPS - 1, pairs[GROUPS - 1])
    image_next = image(1, z_copies)
    next_slice = next_out[...]

    layer_tile2[0] = fold(next_slice * image_next)
    copies = [
        send(layer_tile2.at[0], layer_tile2.at[k], layer_send.at[1, k], layer_recv.at[1, k], (sec, mpo_peer[k]))
        for k in range(1, layers)
    ]
    for copy in copies:
        copy.wait_recv()
    sec_tile2[0] = tree([layer_tile2[k] for k in range(layers)])
    copies = [
        send(sec_tile2.at[0], sec_tile2.at[k], sec_send.at[1, k], sec_recv.at[1, k], (sec_peer[k], mpo))
        for k in range(1, devices)
    ]
    for copy in copies:
        copy.wait_recv()
    alpha_next = total(tree([sec_tile2[k] for k in range(devices)])) * (1.0 / entries)
    first_slice = first[:, pl.ds(pl.multiple_of(mpo * rows, rows), rows), :] * scale
    rest_out[...] = image_next - alpha_next[None] * next_slice - beta[None] * first_slice
    coef_out[0] = jnp.max(alpha_first)
    coef_out[1] = jnp.max(beta)
    coef_out[2] = jnp.max(alpha_next)
    for copy in started:
        copy.wait_send()


def shards(wavefunction, left_size, right_size, right_sector, left_environment, right_environment, term_weights):
    blocks, width = wavefunction.shape[0], wavefunction.shape[1]
    terms = left_environment.shape[0]
    devices = lax.axis_size("sec")
    layers = lax.axis_size("mpo")
    depth = layers // 2
    rows = width // layers
    average = blocks // devices
    capacity = average + max(1, average // 2)
    dma = pltpu.SemaphoreType.DMA
    vmem = pl.BlockSpec(memory_space=pltpu.VMEM)
    smem = pl.BlockSpec(memory_space=pltpu.SMEM)
    return pl.pallas_call(
        functools.partial(kernel, devices, layers, capacity),
        out_shape=(
            jax.ShapeDtypeStruct((blocks, rows, width), F32),
            jax.ShapeDtypeStruct((blocks, rows, width), F32),
            jax.ShapeDtypeStruct((3,), F32),
        ),
        in_specs=[vmem, smem, smem, smem, vmem, vmem, smem],
        out_specs=(vmem, vmem, smem),
        scratch_shapes=[
            pltpu.VMEM((devices - 1, terms, capacity, width, width), BF16),
            pltpu.VMEM((terms, (devices - 1) * capacity + blocks, width, width), BF16),
            pltpu.SMEM((blocks,), jnp.int32),
            pltpu.VMEM((blocks, width, width), F32),
            pltpu.VMEM((blocks, width, terms * width), BF16),
            pltpu.VMEM((blocks, rows, width), F32),
            pltpu.VMEM((2, 2, depth, blocks, rows, width), F32),
            pltpu.VMEM((2, depth, blocks, rows, width), F32),
            pltpu.VMEM((2, depth - 1, blocks * rows, width), BF16),
            pltpu.VMEM((2, depth - 1, blocks * rows, width), BF16),
            pltpu.VMEM((layers, blocks * rows, width), BF16),
            pltpu.VMEM((devices, 8, width), F32),
            pltpu.VMEM((layers, 4, 8, width), F32),
            pltpu.VMEM((devices, 4, 8, width), F32),
            pltpu.VMEM((layers, 8, width), F32),
            pltpu.VMEM((devices, 8, width), F32),
            dma((devices - 1, terms)), dma((devices - 1, terms)), dma((terms,)),
            dma((devices,)), dma((devices,)),
            dma((2, GROUPS, depth)), dma((2, GROUPS, depth)),
            dma((2, GROUPS, depth)), dma((2, GROUPS, depth)),
            dma((GROUPS, depth)), dma((GROUPS, depth)),
            dma((GROUPS, depth)), dma((GROUPS, depth)),
            dma((2, layers)), dma((2, layers)),
            dma((2, devices)), dma((2, devices)),
        ],
        compiler_params=pltpu.CompilerParams(
            collective_id=0, has_side_effects=True, vmem_limit_bytes=40 * 1024 * 1024
        ),
    )(wavefunction, left_size, right_size, right_sector, left_environment, right_environment, term_weights)


def solution(mesh):
    placed = (
        P("sec", None, None),
        P("sec"),
        P(),
        P(),
        P("mpo", "sec", None, None),
        P("mpo", "sec", None, None),
        P("mpo"),
    )
    return jax.shard_map(
        shards,
        mesh=mesh,
        in_specs=placed,
        out_specs=(P("sec", "mpo", None), P("sec", "mpo", None), P()),
        check_vma=False,
    )
```

time: 301 us -> 78.6 us (0.26)
  waiting for transfers between devices: 173 us -> 0 us
  Pallas kernels: 0 us -> 69.7 us
  blocking collectives: 57.4 us -> 0 us
  other arithmetic: 17.4 us -> 0 us
  between operations: 16.9 us -> 0.66 us
  starting transfers between devices: 12.3 us -> 0 us
  matrix products: 8.4 us -> 0 us
  local copies, waits for them, and re-layouts: 13.8 us -> 7.93 us
    psum x2 -> x0, waiting for transfers between devices: 123 us -> none  [apply_operator(): summed = lax.psum(partial_value, 'mpo')]
    pallas_call x0 -> x1, Pallas kernels: none -> 69.7 us  [shards(): pl.pallas_call(functools.partial(kernel, devices, layers, capacity), out_...]
    all_to_all x3 -> x0, waiting for transfers between devices: 50.3 us -> none  [the longest x2 34.9 us: apply_operator(): lax.all_to_all(summed, 'sec', split_axis=0, concat_axis=0, tiled=True)]
    psum x4 -> x0, blocking collectives: 40.5 us -> none  [the longest x2 19 us: rayleigh(): return lax.psum(jnp.sum(basis_vec * applied_vec), 'sec')]
    all_to_all x1 -> x0, blocking collectives: 16.9 us -> none  [apply_operator(): lax.all_to_all(outgoing, 'sec', split_axis=0, concat_axis=0, tiled=True)]
    all_to_all x3 -> x0, starting transfers between devices: 12.2 us -> none  [the longest x2 7.9 us: apply_operator(): lax.all_to_all(summed, 'sec', split_axis=0, concat_axis=0, tiled=True)]
    gather x6 -> x0, local copies, waits for them, and re-layouts: 11.4 us -> none  [the longest x2 4.04 us: apply_operator(): jnp.take(returned.reshape(devices * capacity, width, width), own_places,...]
    dot_general x4 -> x0, matrix products: 8.4 us -> none  [the longest x2 5.01 us: apply_operator(): jnp.einsum('kwac,wkdc->kad', arrived, right_terms, preferred_element_type...]
  transfers between devices with their start and end apart: 5 -> 0, of which waited for: 5 -> 0; matrix products, arithmetic and copies ran while one was open for 1% -> 0% of each run, Pallas kernels for 0% -> 0%
where the time goes in v1:
time: 78.6 us; the launch traced here: 78.3 us
  Pallas kernels  69.7 us (89%)
  local copies, waits for them, and re-layouts  7.93 us (10%)
    pallas_call x1, Pallas kernels, shards(): pl.pallas_call(functools.partial(kernel, devices, layers, capacity), out_...  69.7 us
    unnamed x17, local copies, waits for them, and re-layouts  7.93 us

profile of v1, /device:TPU:0, one launch (start us, length us, event | category | flops | bytes accessed | tf_op | source)
XLA Modules:
  0.0 78.3 jit_solution(9621970647509899971)
XLA Ops:
  0.6 0.0 copy-start
  0.6 1.2 %copy-done = bf16[2,16,128,128]{3,2,1,0:T(8,128)(2,1)S(1)} copy-done((bf16[2,16,128,128]{3,2,1,0:T(8,128)(2,1)S(1)}, bf16[2,16,128,128]{3,2,1,0:T(8,128)(2,1)}, u32[]{:S(2)}) %copy-start) | copy-done | bytes 1048600
  1.9 0.0 copy-start.1
  1.9 1.2 %copy-done.1 = bf16[2,16,128,128]{3,2,1,0:T(8,128)(2,1)S(1)} copy-done((bf16[2,16,128,128]{3,2,1,0:T(8,128)(2,1)S(1)}, bf16[2,16,128,128]{3,2,1,0:T(8,128)(2,1)}, u32[]{:S(2)}) %copy-start.1) | copy-done | bytes 1048600
  3.1 0.0 copy-start.2
  3.1 1.0 %copy-done.2 = bf16[16,128,128]{2,1,0:T(8,128)(2,1)S(1)} copy-done((bf16[16,128,128]{2,1,0:T(8,128)(2,1)S(1)}, bf16[16,128,128]{2,1,0:T(8,128)(2,1)}, u32[]{:S(2)}) %copy-start.2) | copy-done | bytes 524312
  4.1 0.0 copy-start.3
  4.1 0.7 copy-done.3
  4.8 0.0 copy-start.4
  4.8 0.7 copy-done.4
  5.4 0.0 copy-start.5
  5.4 0.7 copy-done.5
  6.1 0.0 copy-start.6
  6.1 0.7 copy-done.6
  6.7 69.7 %shard_map.94 = (f32[16,16,128]{2,1,0:T(8,128)S(1)}, f32[16,16,128]{2,1,0:T(8,128)S(1)}, f32[3]{0:T(128)S(1)}) custom-call(bf16[16,128,128]{2,1,0:T(8,128)(2,1)S(1)} %copy-done.2, s32[16]{0:T(128)S(1)} %copy-done.3, s32[64]{0:T(128)S(1)} %copy-done.4, s32[64]{0:T(128)S(1)} %copy-done.5, bf16[2,16,128,128]{3,2,1,0:T(8,128)(2,1)S(1)} %copy-done, ...), custom_call_target="tpu_custom_call" | custom-call | tf_op jit(solution)/shard_map/pallas_call | solution.py:365
  76.5 0.7 copy.13
  77.1 0.7 copy.14
  77.8 0.5 copy.15
Async XLA Ops:
  0.6 1.2 %copy-start = (bf16[2,16,128,128]{3,2,1,0:T(8,128)(2,1)S(1)}, bf16[2,16,128,128]{3,2,1,0:T(8,128)(2,1)}, u32[]{:S(2)}) copy-start(bf16[2,16,128,128]{3,2,1,0:T(8,128)(2,1)} %left_env.1) | copy-start | bytes 3145732
  1.9 1.2 %copy-start.1 = (bf16[2,16,128,128]{3,2,1,0:T(8,128)(2,1)S(1)}, bf16[2,16,128,128]{3,2,1,0:T(8,128)(2,1)}, u32[]{:S(2)}) copy-start(bf16[2,16,128,128]{3,2,1,0:T(8,128)(2,1)} %right_env.1) | copy-start | bytes 3145732
  3.1 1.0 %copy-start.2 = (bf16[16,128,128]{2,1,0:T(8,128)(2,1)S(1)}, bf16[16,128,128]{2,1,0:T(8,128)(2,1)}, u32[]{:S(2)}) copy-start(bf16[16,128,128]{2,1,0:T(8,128)(2,1)} %wave.1) | copy-start | bytes 1572868
  4.1 0.7 copy-start.3
  4.8 0.7 copy-start.4
  5.4 0.7 copy-start.5
  6.1 0.7 copy-start.6

commit v2 on v1

v2 whole, which is shorter than its diff:
```python
import functools

import jax
import jax.numpy as jnp
from jax import lax
from jax.experimental import pallas as pl
from jax.experimental.pallas import tpu as pltpu
from jax.sharding import PartitionSpec as P

F32 = jnp.float32
BF16 = jnp.bfloat16
GROUPS = 2
UNROLL = 4


def flip(index, mask, size):
    out = index
    bit = 1
    while bit < size:
        if mask & bit:
            out = out + bit * (1 - 2 * ((index // bit) % 2))
        bit *= 2
    return out


def tree(values):
    values = list(values)
    while len(values) > 1:
        values = [values[i] + values[i + 1] for i in range(0, len(values), 2)]
    return values[0]


def fold(x):
    return jnp.sum(x.reshape(-1, 8, x.shape[-1]), axis=0)


def total(tile):
    return jnp.sum(jnp.sum(tile, axis=1, keepdims=True), axis=0, keepdims=True)


def kernel(
    devices, layers, capacity,
    wave_hbm, left_size_hbm, right_size_hbm, right_sector_hbm, left_hbm, right_hbm, weights_hbm,
    next_out, rest_out, coef_out,
    wave, left_size, right_size, right_sector, left_env, right_env, weights,
    staged, held, place, source, valid, first, half, mask,
    part1, pair_in1, z_out1, z_in1, part2, pair_in2, z_out2, z_in2,
    slot_image, rest, gathered,
    norm_tiles, layer1, sec1, layer2, sec2, layer3, sec3,
    load_sem, env_send, env_recv, norm_send, norm_recv,
    pair_send1, pair_recv1, z_send1, z_recv1, pair_send2, pair_recv2, z_send2, z_recv2,
    gather_send, gather_recv, relay_send, relay_recv,
    layer_send, layer_recv, sec_send, sec_recv,
):
    blocks, width = wave.shape[0], wave.shape[1]
    terms = left_env.shape[0]
    depth = layers // 2
    rows = width // layers
    per_group = blocks // GROUPS
    entries = float(blocks * devices * width * width)
    sec = lax.axis_index("sec")
    mpo = lax.axis_index("mpo")
    z, core = mpo // 2, mpo % 2
    partner = 2 * z + 1 - core
    sec_peer = [flip(sec, k, devices) for k in range(devices)]
    mpo_peer = [flip(mpo, k, layers) for k in range(layers)]
    z_peer = [flip(z, k, depth) for k in range(depth)]
    order = list(range(depth - 1, 0, -1))
    started = []

    def send(src, dst, send_sem, recv_sem, to):
        copy = pltpu.make_async_remote_copy(
            src_ref=src, dst_ref=dst, send_sem=send_sem, recv_sem=recv_sem,
            device_id=to, device_id_type=pl.DeviceIdType.MESH,
        )
        copy.start()
        started.append(copy)
        return copy

    loads = []
    pairs_of_refs = (
        (left_size_hbm, left_size), (right_size_hbm, right_size), (right_sector_hbm, right_sector),
        (weights_hbm, weights), (wave_hbm, wave), (right_hbm, right_env), (left_hbm, left_env),
    )
    for n, (src, dst) in enumerate(pairs_of_refs):
        copy = pltpu.make_async_copy(src, dst, load_sem.at[n])
        copy.start()
        loads.append(copy)

    barrier = pltpu.get_barrier_semaphore()
    for k in range(1, devices):
        pl.semaphore_signal(barrier, inc=1, device_id=(sec_peer[k], mpo), device_id_type=pl.DeviceIdType.MESH)
    for k in range(1, layers):
        pl.semaphore_signal(barrier, inc=1, device_id=(sec, mpo_peer[k]), device_id_type=pl.DeviceIdType.MESH)
    for copy in loads[:4]:
        copy.wait()

    def wanted(k):
        base = sec_peer[k] * blocks
        count = jnp.int32(0)
        found = [jnp.int32(0)] * capacity
        for i in range(blocks):
            local = right_sector[base + i] - sec * blocks
            mine = (local >= 0) & (local < blocks)
            found = [jnp.where(mine & (count == c), local, found[c]) for c in range(capacity)]
            count = count + mine.astype(jnp.int32)
        return found

    row_ids = lax.broadcasted_iota(jnp.int32, (width, width), 0)
    col_ids = lax.broadcasted_iota(jnp.int32, (width, width), 1)
    slice_rows = lax.broadcasted_iota(jnp.int32, (rows, width), 0) + mpo * rows
    slice_cols = lax.broadcasted_iota(jnp.int32, (rows, width), 1)

    def masked_block(l, acc):
        live_rows = left_size[l]
        live_cols = right_size[right_sector[sec * blocks + l]]
        live = (row_ids < live_rows) & (col_ids < live_cols)
        block = jnp.where(live, wave[l].astype(F32), 0.0)
        first[l] = block
        live = (slice_rows < live_rows) & (slice_cols < live_cols)
        mask[l] = jnp.where(live, 1.0, 0.0)
        return acc + fold(block * block)

    loads[4].wait()

    def masked_blocks(i, acc):
        for u in range(UNROLL):
            acc = masked_block(i * UNROLL + u, acc)
        return acc

    norm_tiles[0] = lax.fori_loop(0, blocks // UNROLL, masked_blocks, jnp.zeros((8, width), F32))
    pl.semaphore_wait(barrier, devices - 1 + layers - 1)
    norm_copies = [
        send(norm_tiles.at[0], norm_tiles.at[k], norm_send.at[k], norm_recv.at[k], (sec_peer[k], mpo))
        for k in range(1, devices)
    ]

    peers = sorted(range(1, devices), key=lambda k: (bin(k).count("1"), k))
    piece = 2 if capacity % 2 == 0 else capacity
    pieces = capacity // piece
    tables = {k: wanted(k) for k in peers}
    loads[5].wait()
    near = [k for k in peers if bin(k).count("1") == 1]
    far = [k for k in peers if bin(k).count("1") > 1]
    env_copies = {}
    for batch in (near, far):
        for p in range(pieces):
            for k in batch:
                for c in range(p * piece, (p + 1) * piece):
                    for t in range(terms):
                        staged[k - 1, c, t] = right_env[t, tables[k][c]]
                span = pl.ds(p * piece, piece)
                env_copies[k, p] = send(
                    staged.at[k - 1, span], held.at[k - 1, span],
                    env_send.at[k - 1, p], env_recv.at[k - 1, p], (sec_peer[k], mpo),
                )

    own = wanted(0)
    for k in range(devices):
        count = jnp.int32(0)
        found = [jnp.int32(0)] * capacity
        for i in range(blocks):
            sector = right_sector[sec * blocks + i] - sec_peer[k] * blocks
            match = (sector >= 0) & (sector < blocks)
            found = [jnp.where(match & (count == c), i, found[c]) for c in range(capacity)]
            at = k * capacity + jnp.minimum(count, capacity - 1)
            place[i] = at if k == 0 else jnp.where(match, at, place[i])
            count = count + match.astype(jnp.int32)
        for c in range(capacity):
            source[k * capacity + c] = found[c]
            valid[k * capacity + c] = (count > c).astype(jnp.int32)

    for copy in norm_copies:
        copy.wait_recv()
    start_total = total(tree([norm_tiles[k] for k in range(devices)]))
    scale = 1.0 / jnp.sqrt(start_total * (1.0 / entries) + 1e-6)

    def left_block(l, v):
        stacked = jnp.concatenate([left_env[t, l] for t in range(terms)], axis=0)
        product = jnp.dot(stacked, v, preferred_element_type=F32)
        half[l] = jnp.concatenate(
            [(weights[t] * product[t * width:(t + 1) * width]).astype(BF16) for t in range(terms)], axis=1
        )

    def right_product(left, right):
        return lax.dot_general(
            left, jnp.concatenate(right, axis=1), (((1,), (1,)), ((), ())), preferred_element_type=F32
        )

    def loop_blocks(begin, end, body, carry=None):
        def several(i, carry):
            for u in range(UNROLL):
                carry = body(begin + i * UNROLL + u, carry)
            return carry
        return lax.fori_loop(0, (end - begin) // UNROLL, several, carry)

    def put(part, at, out):
        for m in range(layers):
            part[m % 2, m // 2, at] = out[m * rows:(m + 1) * rows]

    class Sum:
        def __init__(self, part, pair_in, z_out, z_in, sems):
            self.part, self.pair_in, self.z_out, self.z_in = part, pair_in, z_out, z_in
            self.pair_send, self.pair_recv, self.z_send, self.z_recv = sems
            self.pairs, self.zs, self.spans = {}, {}, {}

        def begin(self, g, lo, count):
            span = pl.ds(lo, count)
            self.spans[g] = (lo, count)
            self.pairs[g] = {
                k: send(
                    self.part.at[1 - core, z_peer[k], span], self.pair_in.at[k, span],
                    self.pair_send.at[g, k], self.pair_recv.at[g, k], (sec, partner),
                )
                for k in order + [0]
            }

        def middle(self, g):
            lo, count = self.spans[g]
            span, flat = pl.ds(lo, count), pl.ds(lo * rows, count * rows)
            self.zs[g] = []
            for k in order:
                self.pairs[g][k].wait_recv()
                both = self.part[core, z_peer[k], span] + self.pair_in[k, span]
                self.z_out[k - 1, flat] = both.reshape(count * rows, width).astype(BF16)
                self.zs[g].append(send(
                    self.z_out.at[k - 1, flat], self.z_in.at[k - 1, flat],
                    self.z_send.at[g, k - 1], self.z_recv.at[g, k - 1], (sec, 2 * z_peer[k] + core),
                ))
            self.pairs[g][0].wait_recv()

        def end(self, g):
            lo, count = self.spans[g]
            span, flat = pl.ds(lo, count), pl.ds(lo * rows, count * rows)
            value = self.part[core, z, span] + self.pair_in[0, span]
            for copy in self.zs[g]:
                copy.wait_recv()
            for k in range(1, depth):
                value = value + self.z_in[k - 1, flat].astype(F32).reshape(count, rows, width)
            return value

    def spread(n, tiles_layer, tiles_sec, combine):
        copies = [
            send(tiles_layer.at[0], tiles_layer.at[k], layer_send.at[n, k], layer_recv.at[n, k], (sec, mpo_peer[k]))
            for k in range(1, layers)
        ]

        def onward():
            for copy in copies:
                copy.wait_recv()
            combine(tiles_layer, layers, tiles_sec)
            return [
                send(tiles_sec.at[0], tiles_sec.at[k], sec_send.at[n, k], sec_recv.at[n, k], (sec_peer[k], mpo))
                for k in range(1, devices)
            ]
        return onward

    loads[6].wait()

    def first_left(l, carry):
        left_block(l, (first[l] * scale).astype(BF16))
        return carry

    loop_blocks(0, blocks, first_left)
    sum1 = Sum(part1, pair_in1, z_out1, z_in1, (pair_send1, pair_recv1, z_send1, z_recv1))
    inner = jnp.zeros((8, width), F32)
    largest = jnp.zeros((8, width), F32)
    groups = [(0, 0, capacity)] + [(k, 0, capacity) for k in peers[:-1]]
    last = peers[-1]
    groups += [(last, 0, capacity - piece), (last, capacity - piece, capacity)] if pieces > 1 else [(last, 0, capacity)]
    for g, (k, lo, hi) in enumerate(groups):
        if k > 0:
            for p in range(lo // piece, hi // piece):
                env_copies[k, p].wait_recv()
        for c in range(lo, hi):
            at = k * capacity + c
            l = source[at]
            right = [right_env[t, own[c]] if k == 0 else held[k - 1, c, t] for t in range(terms)]
            out = right_product(half[l], right)
            put(part1, at, out)
            live = valid[at] > 0
            start = first[l]
            inner = inner + jnp.where(live, fold(start * out), 0.0)
            top = jnp.max(jnp.abs(out).reshape(-1, 8, width), axis=0)
            largest = jnp.maximum(largest, jnp.where(live, top, 0.0))
        sum1.begin(g, k * capacity + lo, hi - lo)
        if g > 0:
            sum1.middle(g - 1)

    def combine1(tiles, n, into):
        into[0, 0] = tree([tiles[k, 0] for k in range(n)])
        into[0, 1] = functools.reduce(jnp.maximum, [tiles[k, 1] for k in range(n)])

    layer1[0, 0] = inner * scale
    layer1[0, 1] = largest
    onward = spread(0, layer1, sec1, combine1)
    sum1.middle(len(groups) - 1)
    copies = onward()
    for g, (k, lo, hi) in enumerate(groups):
        slot_image[pl.ds(k * capacity + lo, hi - lo)] = sum1.end(g)
    for copy in copies:
        copy.wait_recv()
    alpha_first = total(tree([sec1[k, 0] for k in range(devices)])) * (1.0 / entries)
    peak = functools.reduce(jnp.maximum, [sec1[k, 1] for k in range(devices)])
    peak = jnp.max(jnp.max(peak, axis=1, keepdims=True), axis=0, keepdims=True)
    peak = jnp.maximum(peak, 1e-30)
    shrink = 1.0 / peak
    own_rows = pl.ds(pl.multiple_of(mpo * rows, rows), rows)
    for l in range(blocks):
        rest[l] = mask[l] * slot_image[place[l]] - alpha_first * (first[l, own_rows] * scale)
    value = rest[...]
    gathered[mpo] = (value * shrink[None]).reshape(blocks * rows, width).astype(BF16)

    def flat(g):
        return pl.ds(g * per_group * rows, per_group * rows)

    direct, relayed = {}, {}
    for g in range(GROUPS):
        for k in order:
            direct[g, k] = send(
                gathered.at[mpo, flat(g)], gathered.at[mpo, flat(g)],
                gather_send.at[g, k], gather_recv.at[g, k], (sec, 2 * z_peer[k] + core),
            )
        relayed[g, 0] = send(
            gathered.at[mpo, flat(g)], gathered.at[mpo, flat(g)],
            relay_send.at[g, 0], relay_recv.at[g, 0], (sec, partner),
        )

    def combine(tiles, n, into):
        into[0] = tree([tiles[k] for k in range(n)])

    layer2[0] = fold(value * value)
    beta_onward = spread(1, layer2, sec2, combine)

    def next_block(l):
        if rows % 16 == 0:
            pieces = [gathered[m, pl.ds(pl.multiple_of(l * rows, rows), rows)] for m in range(layers)]
            return jnp.concatenate(pieces, axis=0)
        pieces = [
            gathered[m, pl.ds((l * rows) // 16 * 16, 16)].astype(F32)[(l * rows) % 16:(l * rows) % 16 + rows]
            for m in range(layers)
        ]
        return jnp.concatenate(pieces, axis=0).astype(BF16)

    def second_left(l, carry):
        left_block(l, next_block(l))
        return carry

    def second_right(l, inner):
        at = place[l]
        right = [held[at // capacity, lax.rem(at, capacity), t] for t in range(terms)]
        out = right_product(half[l], right)
        put(part2, l, out)
        return inner + fold(next_block(l).astype(F32) * out)

    sum2 = Sum(part2, pair_in2, z_out2, z_in2, (pair_send2, pair_recv2, z_send2, z_recv2))
    for c in range(capacity):
        for t in range(terms):
            held[devices - 1, c, t] = right_env[t, own[c]]
    for l in range(blocks):
        at = place[l]
        place[l] = jnp.where(at < capacity, at + (devices - 1) * capacity, at - capacity)
    inner = jnp.zeros((8, width), F32)
    for g in range(GROUPS):
        for k in reversed(order):
            direct[g, k].wait_recv()
            from_there = 2 * z_peer[k] + core
            relayed[g, k] = send(
                gathered.at[from_there, flat(g)], gathered.at[from_there, flat(g)],
                relay_send.at[g, k], relay_recv.at[g, k], (sec, partner),
            )
        if g == 0:
            copies = beta_onward()
        for k in [0] + order[::-1]:
            relayed[g, k].wait_recv()
        begin, end = g * per_group, (g + 1) * per_group
        if rows % 16 == 0:
            loop_blocks(begin, end, second_left)
            inner = loop_blocks(begin, end, second_right, inner)
        else:
            for l in range(begin, end):
                second_left(l, None)
                inner = second_right(l, inner)
        sum2.begin(g, begin, per_group)
        if g > 0:
            sum2.middle(g - 1)
    layer3[0] = inner
    onward = spread(2, layer3, sec3, combine)
    sum2.middle(GROUPS - 1)
    for copy in copies:
        copy.wait_recv()
    rest_total = total(tree([sec2[k] for k in range(devices)]))
    beta = jnp.sqrt(rest_total * (1.0 / entries) + 1e-6)
    next_out[...] = rest[...] / beta[None]
    copies = onward()
    grow = peak / beta
    first_slice = first[:, own_rows, :] * scale
    for copy in copies:
        copy.wait_recv()
    alpha_next = total(tree([sec3[k] for k in range(devices)])) * (1.0 / entries) * grow * grow
    rest_out[...] = -alpha_next[None] * next_out[...] - beta[None] * first_slice
    coef_out[0] = jnp.max(alpha_first)
    coef_out[1] = jnp.max(beta)
    coef_out[2] = jnp.max(alpha_next)
    for g in range(GROUPS):
        span = pl.ds(g * per_group, per_group)
        rest_out[span] = rest_out[span] + mask[span] * sum2.end(g) * grow[None]
    for copy in started:
        copy.wait_send()


def shards(wavefunction, left_size, right_size, right_sector, left_environment, right_environment, term_weights):
    blocks, width = wavefunction.shape[0], wavefunction.shape[1]
    terms = left_environment.shape[0]
    devices = lax.axis_size("sec")
    layers = lax.axis_size("mpo")
    depth = layers // 2
    rows = width // layers
    average = blocks // devices
    capacity = average + max(1, average // 2)
    slots = devices * capacity
    dma = pltpu.SemaphoreType.DMA
    vmem = pl.BlockSpec(memory_space=pltpu.VMEM)
    smem = pl.BlockSpec(memory_space=pltpu.SMEM)
    hbm = pl.BlockSpec(memory_space=pl.ANY)

    def sum_scratch(count):
        return [
            pltpu.VMEM((2, depth, count, rows, width), F32),
            pltpu.VMEM((depth, count, rows, width), F32),
            pltpu.VMEM((depth - 1, count * rows, width), BF16),
            pltpu.VMEM((depth - 1, count * rows, width), BF16),
        ]

    many = devices + 1
    return pl.pallas_call(
        functools.partial(kernel, devices, layers, capacity),
        out_shape=(
            jax.ShapeDtypeStruct((blocks, rows, width), F32),
            jax.ShapeDtypeStruct((blocks, rows, width), F32),
            jax.ShapeDtypeStruct((3,), F32),
        ),
        in_specs=[hbm] * 7,
        out_specs=(vmem, vmem, smem),
        scratch_shapes=[
            pltpu.VMEM(wavefunction.shape, BF16),
            pltpu.SMEM(left_size.shape, jnp.int32),
            pltpu.SMEM(right_size.shape, jnp.int32),
            pltpu.SMEM(right_sector.shape, jnp.int32),
            pltpu.VMEM(left_environment.shape, BF16),
            pltpu.VMEM(right_environment.shape, BF16),
            pltpu.SMEM(term_weights.shape, F32),
            pltpu.VMEM((devices - 1, capacity, terms, width, width), BF16),
            pltpu.VMEM((devices, capacity, terms, width, width), BF16),
            pltpu.SMEM((blocks,), jnp.int32),
            pltpu.SMEM((slots,), jnp.int32),
            pltpu.SMEM((slots,), jnp.int32),
            pltpu.VMEM((blocks, width, width), F32),
            pltpu.VMEM((blocks, width, terms * width), BF16),
            pltpu.VMEM((blocks, rows, width), F32),
            *sum_scratch(slots),
            *sum_scratch(blocks),
            pltpu.VMEM((slots, rows, width), F32),
            pltpu.VMEM((blocks, rows, width), F32),
            pltpu.VMEM((layers, blocks * rows, width), BF16),
            pltpu.VMEM((devices, 8, width), F32),
            pltpu.VMEM((layers, 2, 8, width), F32),
            pltpu.VMEM((devices, 2, 8, width), F32),
            pltpu.VMEM((layers, 8, width), F32),
            pltpu.VMEM((devices, 8, width), F32),
            pltpu.VMEM((layers, 8, width), F32),
            pltpu.VMEM((devices, 8, width), F32),
            dma((7,)),
            dma((devices - 1, capacity)), dma((devices - 1, capacity)),
            dma((devices,)), dma((devices,)),
            dma((many, depth)), dma((many, depth)), dma((many, depth)), dma((many, depth)),
            dma((GROUPS, depth)), dma((GROUPS, depth)), dma((GROUPS, depth)), dma((GROUPS, depth)),
            dma((GROUPS, depth)), dma((GROUPS, depth)),
            dma((GROUPS, depth)), dma((GROUPS, depth)),
            dma((3, layers)), dma((3, layers)),
            dma((3, devices)), dma((3, devices)),
        ],
        compiler_params=pltpu.CompilerParams(
            collective_id=0, has_side_effects=True, vmem_limit_bytes=58 * 1024 * 1024
        ),
    )(wavefunction, left_size, right_size, right_sector, left_environment, right_environment, term_weights)


def solution(mesh):
    placed = (
        P("sec", None, None),
        P("sec"),
        P(),
        P(),
        P("mpo", "sec", None, None),
        P("mpo", "sec", None, None),
        P("mpo"),
    )
    return jax.shard_map(
        shards,
        mesh=mesh,
        in_specs=placed,
        out_specs=(P("sec", "mpo", None), P("sec", "mpo", None), P()),
        check_vma=False,
    )
```

time: 78.6 us -> 61.4 us (0.78)
  Pallas kernels: 69.7 us -> 57.8 us
  local copies, waits for them, and re-layouts: 7.93 us -> 2.79 us
    pallas_call x1, Pallas kernels: 69.7 us -> 57.8 us  [shards(): pl.pallas_call(functools.partial(kernel, devices, layers, capacity), out_...]
    unnamed x17 -> x7, local copies, waits for them, and re-layouts: 7.93 us -> 2.79 us
where the time goes in v2:
time: 61.4 us; the launch traced here: 61.2 us
  Pallas kernels  57.8 us (94%)
  local copies, waits for them, and re-layouts  2.79 us (5%)
  between operations  0.65 us (1%)
    pallas_call x1, Pallas kernels, shards(): pl.pallas_call(functools.partial(kernel, devices, layers, capacity), out_...  57.8 us
    unnamed x7, local copies, waits for them, and re-layouts  2.79 us

profile of v2, /device:TPU:0, one launch (start us, length us, event | category | flops | bytes accessed | tf_op | source)
XLA Modules:
  0.0 61.2 jit_solution(11343942741913821270)
XLA Ops:
  0.6 57.8 %shard_map.94 = (f32[16,16,128]{2,1,0:T(8,128)}, f32[16,16,128]{2,1,0:T(8,128)}, f32[3]{0:T(128)}) custom-call(bf16[16,128,128]{2,1,0:T(8,128)(2,1)} %wave_hbm.1, s32[16]{0:T(128)} %left_size_hbm.1, s32[64]{0:T(128)} %right_size_hbm.1, s32[64]{0:T(128)} %right_sector_hbm.1, bf16[2,16,128,128]{3,2,1,0:T(8,128)(2,1)} %left_hbm.1, ...), custom_call_target="tpu_custom_call" | custom-call | tf_op jit(solution)/shard_map/pallas_call | solution.py:436
  58.4 0.0 copy-start
  58.4 1.6 %copy.13 = f32[16,16,128]{2,1,0:T(8,128)} copy(f32[16,16,128]{2,1,0:T(8,128)} %get-tuple-element.6) | data formatting | bytes 262144
  60.0 0.0 copy-done
  60.0 0.0 copy-start.1
  60.0 0.7 %copy.14 = f32[16,16,128]{2,1,0:T(8,128)} copy(f32[16,16,128]{2,1,0:T(8,128)S(1)} %copy-done) | data formatting | bytes 262144
  60.7 0.0 copy-done.1
  60.7 0.5 copy.15
Async XLA Ops:
  58.4 1.6 %copy-start = (f32[16,16,128]{2,1,0:T(8,128)S(1)}, f32[16,16,128]{2,1,0:T(8,128)}, u32[]{:S(2)}) copy-start(f32[16,16,128]{2,1,0:T(8,128)} %get-tuple-element.7) | copy-start | bytes 393220
  60.0 0.7 %copy-start.1 = (f32[3]{0:T(128)S(1)}, f32[3]{0:T(128)}, u32[]{:S(2)}) copy-start(f32[3]{0:T(128)} %get-tuple-element.8) | copy-start | bytes 40

commit v3 on v2

--- a/solution.py
+++ b/solution.py
@@ -9,7 +9,6 @@
 
 F32 = jnp.float32
 BF16 = jnp.bfloat16
-GROUPS = 2
 UNROLL = 4
 
 
@@ -43,10 +42,10 @@
     wave_hbm, left_size_hbm, right_size_hbm, right_sector_hbm, left_hbm, right_hbm, weights_hbm,
     next_out, rest_out, coef_out,
     wave, left_size, right_size, right_sector, left_env, right_env, weights,
-    staged, held, place, source, valid, first, half, mask,
+    staged, held, pool, place, slot_of, left_of, first, half, mask, first_rows,
     part1, pair_in1, z_out1, z_in1, part2, pair_in2, z_out2, z_in2,
-    slot_image, rest, gathered,
-    norm_tiles, layer1, sec1, layer2, sec2, layer3, sec3,
+    image, image2, rest, gathered,
+    norm_tiles, layer0, layer1, sec1, layer2, sec2, layer3, sec3,
     load_sem, env_send, env_recv, norm_send, norm_recv,
     pair_send1, pair_recv1, z_send1, z_recv1, pair_send2, pair_recv2, z_send2, z_recv2,
     gather_send, gather_recv, relay_send, relay_recv,
@@ -56,7 +55,6 @@
     terms = left_env.shape[0]
     depth = layers // 2
     rows = width // layers
-    per_group = blocks // GROUPS
     entries = float(blocks * devices * width * width)
     sec = lax.axis_index("sec")
     mpo = lax.axis_index("mpo")
@@ -92,6 +90,8 @@
         pl.semaphore_signal(barrier, inc=1, device_id=(sec_peer[k], mpo), device_id_type=pl.DeviceIdType.MESH)
     for k in range(1, layers):
         pl.semaphore_signal(barrier, inc=1, device_id=(sec, mpo_peer[k]), device_id_type=pl.DeviceIdType.MESH)
+    for c in range(capacity, devices * capacity):
+        pool[c] = jnp.zeros(pool.shape[1:], BF16)
     for copy in loads[:4]:
         copy.wait()
 
@@ -128,7 +128,18 @@
             acc = masked_block(i * UNROLL + u, acc)
         return acc
 
-    norm_tiles[0] = lax.fori_loop(0, blocks // UNROLL, masked_blocks, jnp.zeros((8, width), F32))
+    norm_tiles[0, 0] = lax.fori_loop(0, blocks // UNROLL, masked_blocks, jnp.zeros((8, width), F32))
+    loads[5].wait()
+
+    def top(x):
+        return jnp.max(jnp.abs(x).astype(F32).reshape(-1, 8, x.shape[-1]), axis=0)
+
+    def largest_right(l, acc):
+        for t in range(terms):
+            acc = jnp.maximum(acc, top(right_env[t, l]))
+        return acc
+
+    norm_tiles[0, 1] = lax.fori_loop(0, blocks, largest_right, jnp.zeros((8, width), F32))
     pl.semaphore_wait(barrier, devices - 1 + layers - 1)
     norm_copies = [
         send(norm_tiles.at[0], norm_tiles.at[k], norm_send.at[k], norm_recv.at[k], (sec_peer[k], mpo))
@@ -139,7 +150,6 @@
     piece = 2 if capacity % 2 == 0 else capacity
     pieces = capacity // piece
     tables = {k: wanted(k) for k in peers}
-    loads[5].wait()
     near = [k for k in peers if bin(k).count("1") == 1]
     far = [k for k in peers if bin(k).count("1") > 1]
     env_copies = {}
@@ -156,23 +166,43 @@
                 )
 
     own = wanted(0)
+
+    def arrival(k, c):
+        if k == 0:
+            return c
+        batch, start = (near, capacity) if k in near else (far, capacity * (1 + len(near)))
+        return start + (c // piece) * (len(batch) * piece) + batch.index(k) * piece + lax.rem(c, jnp.int32(piece))
+
+    slots = [jnp.int32(0)] * blocks
     for k in range(devices):
         count = jnp.int32(0)
-        found = [jnp.int32(0)] * capacity
         for i in range(blocks):
             sector = right_sector[sec * blocks + i] - sec_peer[k] * blocks
             match = (sector >= 0) & (sector < blocks)
-            found = [jnp.where(match & (count == c), i, found[c]) for c in range(capacity)]
-            at = k * capacity + jnp.minimum(count, capacity - 1)
-            place[i] = at if k == 0 else jnp.where(match, at, place[i])
+            slots[i] = jnp.where(match, arrival(k, jnp.minimum(count, capacity - 1)), slots[i])
             count = count + match.astype(jnp.int32)
-        for c in range(capacity):
-            source[k * capacity + c] = found[c]
-            valid[k * capacity + c] = (count > c).astype(jnp.int32)
+    ranks = []
+    for i in range(blocks):
+        rank = jnp.int32(0)
+        for j in range(blocks):
+            if j != i:
+                rank = rank + (slots[j] < slots[i]).astype(jnp.int32)
+        ranks.append(rank)
+        place[i] = rank
+    for q in range(blocks):
+        slot, left = jnp.int32(0), jnp.int32(0)
+        for i in range(blocks):
+            slot = jnp.where(ranks[i] == q, slots[i], slot)
+            left = jnp.where(ranks[i] == q, i, left)
+        slot_of[q] = slot
+        left_of[q] = left
+    for c in range(capacity):
+        for t in range(terms):
+            pool[c, t] = right_env[t, own[c]]
 
     for copy in norm_copies:
         copy.wait_recv()
-    start_total = total(tree([norm_tiles[k] for k in range(devices)]))
+    start_total = total(tree([norm_tiles[k, 0] for k in range(devices)]))
     scale = 1.0 / jnp.sqrt(start_total * (1.0 / entries) + 1e-6)
 
     def left_block(l, v):
@@ -257,154 +287,182 @@
 
     loads[6].wait()
 
-    def first_left(l, carry):
+    def first_left(l, acc):
         left_block(l, (first[l] * scale).astype(BF16))
-        return carry
-
-    loop_blocks(0, blocks, first_left)
+        return jnp.maximum(acc, top(half[l][:, :width])) if terms == 1 else jnp.maximum(
+            acc, functools.reduce(jnp.maximum, [top(half[l][:, t * width:(t + 1) * width]) for t in range(terms)])
+        )
+
+    layer0[0, 0] = loop_blocks(0, blocks, first_left, jnp.zeros((8, width), F32))
+    layer0[0, 1] = functools.reduce(jnp.maximum, [norm_tiles[k, 1] for k in range(devices)])
+    scale_copies = [
+        send(layer0.at[0], layer0.at[k], layer_send.at[3, k], layer_recv.at[3, k], (sec, mpo_peer[k]))
+        for k in range(1, layers)
+    ]
+    own_rows = pl.ds(pl.multiple_of(mpo * rows, rows), rows)
+    for q in range(blocks):
+        first_rows[q] = first[left_of[q], own_rows] * scale
+
+    batches, taken, begun = [], 0, 0
+    stages = [[(k, p) for k in near] for p in range(pieces)] + [[(k, p) for k in far] for p in range(pieces)]
+    missing = (devices - 1) * capacity
+    waiting = []
+    for n, stage in enumerate(stages):
+        waiting += stage
+        missing -= len(stage) * piece
+        ready = max(0, blocks - missing) // 2 * 2
+        final = n == len(stages) - 1
+        if final or ready - taken >= 4:
+            batches.append((taken, ready - taken, waiting))
+            taken, waiting = ready, []
     sum1 = Sum(part1, pair_in1, z_out1, z_in1, (pair_send1, pair_recv1, z_send1, z_recv1))
-    inner = jnp.zeros((8, width), F32)
-    largest = jnp.zeros((8, width), F32)
-    groups = [(0, 0, capacity)] + [(k, 0, capacity) for k in peers[:-1]]
-    last = peers[-1]
-    groups += [(last, 0, capacity - piece), (last, capacity - piece, capacity)] if pieces > 1 else [(last, 0, capacity)]
-    for g, (k, lo, hi) in enumerate(groups):
-        if k > 0:
-            for p in range(lo // piece, hi // piece):
-                env_copies[k, p].wait_recv()
-        for c in range(lo, hi):
-            at = k * capacity + c
-            l = source[at]
-            right = [right_env[t, own[c]] if k == 0 else held[k - 1, c, t] for t in range(terms)]
-            out = right_product(half[l], right)
-            put(part1, at, out)
-            live = valid[at] > 0
-            start = first[l]
-            inner = inner + jnp.where(live, fold(start * out), 0.0)
-            top = jnp.max(jnp.abs(out).reshape(-1, 8, width), axis=0)
-            largest = jnp.maximum(largest, jnp.where(live, top, 0.0))
-        sum1.begin(g, k * capacity + lo, hi - lo)
-        if g > 0:
-            sum1.middle(g - 1)
-
-    def combine1(tiles, n, into):
-        into[0, 0] = tree([tiles[k, 0] for k in range(n)])
-        into[0, 1] = functools.reduce(jnp.maximum, [tiles[k, 1] for k in range(n)])
-
-    layer1[0, 0] = inner * scale
-    layer1[0, 1] = largest
-    onward = spread(0, layer1, sec1, combine1)
-    sum1.middle(len(groups) - 1)
-    copies = onward()
-    for g, (k, lo, hi) in enumerate(groups):
-        slot_image[pl.ds(k * capacity + lo, hi - lo)] = sum1.end(g)
-    for copy in copies:
+    sum2 = Sum(part2, pair_in2, z_out2, z_in2, (pair_send2, pair_recv2, z_send2, z_recv2))
+    sums = {"inner": jnp.zeros((8, width), F32), "own": jnp.zeros((8, width), F32), "cross": jnp.zeros((8, width), F32)}
+    direct, relayed, peak = {}, {}, []
+
+    def flat(b):
+        lo, count, _ = batches[b]
+        return pl.ds(lo * rows, count * rows)
+
+    def step_right(b):
+        lo, count, pieces_there = batches[b]
+        for k, p in pieces_there:
+            env_copies[k, p].wait_recv()
+            for c in range(p * piece, (p + 1) * piece):
+                batch, start = (near, capacity) if k in near else (far, capacity * (1 + len(near)))
+                at = start + (c // piece) * (len(batch) * piece) + batch.index(k) * piece + c % piece
+                for t in range(terms):
+                    pool[at, t] = held[k - 1, c, t]
+        for q in range(lo, lo + count):
+            l, at = left_of[q], slot_of[q]
+            out = right_product(half[l], [pool[at, t] for t in range(terms)])
+            put(part1, q, out)
+            sums["inner"] = sums["inner"] + fold(first[l] * out)
+        sum1.begin(b, lo, count)
+
+    def step_middle(b):
+        sum1.middle(b)
+
+    def step_gather(b):
+        lo, count, _ = batches[b]
+        if not peak:
+            for copy in scale_copies:
+                copy.wait_recv()
+            for n in range(2):
+                tile = functools.reduce(jnp.maximum, [layer0[k, n] for k in range(layers)])
+                tile = jnp.max(jnp.max(tile, axis=1, keepdims=True), axis=0, keepdims=True)
+                peak.append(jnp.maximum(tile, 1e-18))
+        live = jnp.stack([mask[left_of[q]] for q in range(lo, lo + count)])
+        value = sum1.end(b) * live
+        image[pl.ds(lo, count)] = value
+        small = value * (1.0 / peak[0])[None] * (1.0 / peak[1])[None]
+        gathered[mpo, flat(b)] = small.reshape(count * rows, width).astype(BF16)
+        here = gathered.at[mpo, flat(b)]
+        for k in order:
+            direct[b, k] = send(here, here, gather_send.at[b, k], gather_recv.at[b, k], (sec, 2 * z_peer[k] + core))
+        relayed[b, 0] = send(here, here, relay_send.at[b, 0], relay_recv.at[b, 0], (sec, partner))
+
+    def step_relay(b):
+        for k in reversed(order):
+            direct[b, k].wait_recv()
+            here = gathered.at[2 * z_peer[k] + core, flat(b)]
+            relayed[b, k] = send(here, here, relay_send.at[b, k], relay_recv.at[b, k], (sec, partner))
+
+    def image_block(q):
+        if rows % 16 == 0:
+            return jnp.concatenate([gathered[m, pl.ds(q * rows, rows)] for m in range(layers)], axis=0)
+        low = (q * rows) // 16 * 16
+        cut = q * rows - low
+        blocks16 = [gathered[m, pl.ds(low, 16)].astype(F32)[cut:cut + rows] for m in range(layers)]
+        return jnp.concatenate(blocks16, axis=0).astype(BF16)
+
+    def step_second(b):
+        lo, count, _ = batches[b]
+        for k in [0] + order[::-1]:
+            relayed[b, k].wait_recv()
+        for q in range(lo, lo + count):
+            l, at = left_of[q], slot_of[q]
+            v = image_block(q)
+            stacked = jnp.concatenate([left_env[t, l] for t in range(terms)], axis=0)
+            product = jnp.dot(stacked, v, preferred_element_type=F32)
+            left = jnp.concatenate(
+                [(weights[t] * product[t * width:(t + 1) * width]).astype(BF16) for t in range(terms)], axis=1
+            )
+            out = right_product(left, [pool[at, t] for t in range(terms)])
+            put(part2, q, out)
+            sums["own"] = sums["own"] + fold(v.astype(F32) * out)
+            sums["cross"] = sums["cross"] + fold(first[l] * out)
+        sum2.begin(b, lo, count)
+
+    def step_last(b):
+        sum2.middle(b)
+
+    def combine(tiles, n, into):
+        for c in range(into.shape[1]):
+            into[0, c] = tree([tiles[k, c] for k in range(n)])
+
+    def mean(tiles, c):
+        return total(tree([tiles[k, c] for k in range(devices)])) * (1.0 / entries)
+
+    steps = (step_right, step_middle, step_gather, step_relay, step_second, step_last)
+    offsets = (0.0, 1.5, 3.5, 5.5, 7.0, 8.5)
+    starts = [3.0 * b if b < len(batches) // 2 else 3.0 * b + 2.0 for b in range(len(batches))]
+    plan = sorted(
+        (starts[b] + offsets[i], b, i) for b in range(len(batches)) for i in range(len(steps))
+    )
+    end = len(batches) - 1
+    alpha_first = rest_copies = rest_onward = alpha_copies = None
+    for _, b, i in plan:
+        steps[i](b)
+        if b < end:
+            continue
+        if i == 0:
+            layer1[0, 0] = sums["inner"] * scale
+            onward = spread(0, layer1, sec1, combine)
+        if i == 1:
+            alpha_copies = onward()
+        if i == 2:
+            for copy in alpha_copies:
+                copy.wait_recv()
+            alpha_first = total(tree([sec1[k, 0] for k in range(devices)])) * (1.0 / entries)
+            value = image[...]
+            away = value - alpha_first[None] * first_rows[...]
+            rest[...] = away
+            layer2[0, 0] = fold(away * away)
+            layer2[0, 1] = fold(value * value)
+            rest_onward = spread(1, layer2, sec2, combine)
+        if i == 3:
+            rest_copies = rest_onward()
+        if i == 4:
+            for copy in rest_copies:
+                copy.wait_recv()
+            beta = jnp.sqrt(mean(sec2, 0) + 1e-6)
+            grow = peak[0] * (peak[1] / beta)
+            layer3[0, 0] = sums["own"] * grow * grow
+            layer3[0, 1] = sums["cross"] * scale * grow
+            onward = spread(2, layer3, sec3, combine)
+    image_square = mean(sec2, 1)
+    rest[...] = rest[...] / beta[None]
+    for l in range(blocks):
+        next_out[l] = rest[place[l]]
+    alpha_copies = onward()
+    for b in range(len(batches)):
+        lo, count, _ = batches[b]
+        image2[pl.ds(lo, count)] = sum2.end(b)
+    for copy in alpha_copies:
         copy.wait_recv()
-    alpha_first = total(tree([sec1[k, 0] for k in range(devices)])) * (1.0 / entries)
-    peak = functools.reduce(jnp.maximum, [sec1[k, 1] for k in range(devices)])
-    peak = jnp.max(jnp.max(peak, axis=1, keepdims=True), axis=0, keepdims=True)
-    peak = jnp.maximum(peak, 1e-30)
-    shrink = 1.0 / peak
-    own_rows = pl.ds(pl.multiple_of(mpo * rows, rows), rows)
+    ratio = alpha_first / beta
+    alpha_next = (
+        mean(sec3, 0) - ratio * (image_square / beta) - ratio * mean(sec3, 1)
+        + ratio * ratio * alpha_first
+    )
     for l in range(blocks):
-        rest[l] = mask[l] * slot_image[place[l]] - alpha_first * (first[l, own_rows] * scale)
-    value = rest[...]
-    gathered[mpo] = (value * shrink[None]).reshape(blocks * rows, width).astype(BF16)
-
-    def flat(g):
-        return pl.ds(g * per_group * rows, per_group * rows)
-
-    direct, relayed = {}, {}
-    for g in range(GROUPS):
-        for k in order:
-            direct[g, k] = send(
-                gathered.at[mpo, flat(g)], gathered.at[mpo, flat(g)],
-                gather_send.at[g, k], gather_recv.at[g, k], (sec, 2 * z_peer[k] + core),
-            )
-        relayed[g, 0] = send(
-            gathered.at[mpo, flat(g)], gathered.at[mpo, flat(g)],
-            relay_send.at[g, 0], relay_recv.at[g, 0], (sec, partner),
-        )
-
-    def combine(tiles, n, into):
-        into[0] = tree([tiles[k] for k in range(n)])
-
-    layer2[0] = fold(value * value)
-    beta_onward = spread(1, layer2, sec2, combine)
-
-    def next_block(l):
-        if rows % 16 == 0:
-            pieces = [gathered[m, pl.ds(pl.multiple_of(l * rows, rows), rows)] for m in range(layers)]
-            return jnp.concatenate(pieces, axis=0)
-        pieces = [
-            gathered[m, pl.ds((l * rows) // 16 * 16, 16)].astype(F32)[(l * rows) % 16:(l * rows) % 16 + rows]
-            for m in range(layers)
-        ]
-        return jnp.concatenate(pieces, axis=0).astype(BF16)
-
-    def second_left(l, carry):
-        left_block(l, next_block(l))
-        return carry
-
-    def second_right(l, inner):
-        at = place[l]
-        right = [held[at // capacity, lax.rem(at, capacity), t] for t in range(terms)]
-        out = right_product(half[l], right)
-        put(part2, l, out)
-        return inner + fold(next_block(l).astype(F32) * out)
-
-    sum2 = Sum(part2, pair_in2, z_out2, z_in2, (pair_send2, pair_recv2, z_send2, z_recv2))
-    for c in range(capacity):
-        for t in range(terms):
-            held[devices - 1, c, t] = right_env[t, own[c]]
-    for l in range(blocks):
-        at = place[l]
-        place[l] = jnp.where(at < capacity, at + (devices - 1) * capacity, at - capacity)
-    inner = jnp.zeros((8, width), F32)
-    for g in range(GROUPS):
-        for k in reversed(order):
-            direct[g, k].wait_recv()
-            from_there = 2 * z_peer[k] + core
-            relayed[g, k] = send(
-                gathered.at[from_there, flat(g)], gathered.at[from_there, flat(g)],
-                relay_send.at[g, k], relay_recv.at[g, k], (sec, partner),
-            )
-        if g == 0:
-            copies = beta_onward()
-        for k in [0] + order[::-1]:
-            relayed[g, k].wait_recv()
-        begin, end = g * per_group, (g + 1) * per_group
-        if rows % 16 == 0:
-            loop_blocks(begin, end, second_left)
-            inner = loop_blocks(begin, end, second_right, inner)
-        else:
-            for l in range(begin, end):
-                second_left(l, None)
-                inner = second_right(l, inner)
-        sum2.begin(g, begin, per_group)
-        if g > 0:
-            sum2.middle(g - 1)
-    layer3[0] = inner
-    onward = spread(2, layer3, sec3, combine)
-    sum2.middle(GROUPS - 1)
-    for copy in copies:
-        copy.wait_recv()
-    rest_total = total(tree([sec2[k] for k in range(devices)]))
-    beta = jnp.sqrt(rest_total * (1.0 / entries) + 1e-6)
-    next_out[...] = rest[...] / beta[None]
-    copies = onward()
-    grow = peak / beta
-    first_slice = first[:, own_rows, :] * scale
-    for copy in copies:
-        copy.wait_recv()
-    alpha_next = total(tree([sec3[k] for k in range(devices)])) * (1.0 / entries) * grow * grow
-    rest_out[...] = -alpha_next[None] * next_out[...] - beta[None] * first_slice
+        q = place[l]
+        applied = mask[l] * image2[q] * grow - ratio * image[q]
+        rest_out[l] = applied - alpha_next * next_out[l] - beta * first_rows[q]
     coef_out[0] = jnp.max(alpha_first)
     coef_out[1] = jnp.max(beta)
     coef_out[2] = jnp.max(alpha_next)
-    for g in range(GROUPS):
-        span = pl.ds(g * per_group, per_group)
-        rest_out[span] = rest_out[span] + mask[span] * sum2.end(g) * grow[None]
     for copy in started:
         copy.wait_send()
 
@@ -451,33 +509,37 @@
             pltpu.VMEM(right_environment.shape, BF16),
             pltpu.SMEM(term_weights.shape, F32),
             pltpu.VMEM((devices - 1, capacity, terms, width, width), BF16),
-            pltpu.VMEM((devices, capacity, terms, width, width), BF16),
+            pltpu.VMEM((devices - 1, capacity, terms, width, width), BF16),
+            pltpu.VMEM((slots, terms, width, width), BF16),
             pltpu.SMEM((blocks,), jnp.int32),
-            pltpu.SMEM((slots,), jnp.int32),
-            pltpu.SMEM((slots,), jnp.int32),
+            pltpu.SMEM((blocks,), jnp.int32),
+            pltpu.SMEM((blocks,), jnp.int32),
             pltpu.VMEM((blocks, width, width), F32),
             pltpu.VMEM((blocks, width, terms * width), BF16),
             pltpu.VMEM((blocks, rows, width), F32),
-            *sum_scratch(slots),
+            pltpu.VMEM((blocks, rows, width), F32),
             *sum_scratch(blocks),
-            pltpu.VMEM((slots, rows, width), F32),
+            *sum_scratch(blocks),
+            pltpu.VMEM((blocks, rows, width), F32),
+            pltpu.VMEM((blocks, rows, width), F32),
             pltpu.VMEM((blocks, rows, width), F32),
             pltpu.VMEM((layers, blocks * rows, width), BF16),
-            pltpu.VMEM((devices, 8, width), F32),
+            pltpu.VMEM((devices, 2, 8, width), F32),
+            pltpu.VMEM((layers, 2, 8, width), F32),
+            pltpu.VMEM((layers, 1, 8, width), F32),
+            pltpu.VMEM((devices, 1, 8, width), F32),
             pltpu.VMEM((layers, 2, 8, width), F32),
             pltpu.VMEM((devices, 2, 8, width), F32),
-            pltpu.VMEM((layers, 8, width), F32),
-            pltpu.VMEM((devices, 8, width), F32),
-            pltpu.VMEM((layers, 8, width), F32),
-            pltpu.VMEM((devices, 8, width), F32),
+            pltpu.VMEM((layers, 2, 8, width), F32),
+            pltpu.VMEM((devices, 2, 8, width), F32),
             dma((7,)),
             dma((devices - 1, capacity)), dma((devices - 1, capacity)),
             dma((devices,)), dma((devices,)),
             dma((many, depth)), dma((many, depth)), dma((many, depth)), dma((many, depth)),
-            dma((GROUPS, depth)), dma((GROUPS, depth)), dma((GROUPS, depth)), dma((GROUPS, depth)),
-            dma((GROUPS, depth)), dma((GROUPS, depth)),
-            dma((GROUPS, depth)), dma((GROUPS, depth)),
-            dma((3, layers)), dma((3, layers)),
+            dma((many, depth)), dma((many, depth)), dma((many, depth)), dma((many, depth)),
+            dma((many, depth)), dma((many, depth)),
+            dma((many, depth)), dma((many, depth)),
+            dma((4, layers)), dma((4, layers)),
             dma((3, devices)), dma((3, devices)),
         ],
         compiler_params=pltpu.CompilerParams(

time: 61.4 us -> 64.5 us (1.050)
  Pallas kernels: 57.8 us -> 60.9 us
    pallas_call x1, Pallas kernels: 57.8 us -> 60.9 us  [shards(): pl.pallas_call(functools.partial(kernel, devices, layers, capacity), out_...]
where the time goes in v3:
time: 64.5 us; the launch traced here: 64.3 us
  Pallas kernels  60.9 us (94%)
  local copies, waits for them, and re-layouts  2.79 us (4%)
  between operations  0.65 us (1%)
    pallas_call x1, Pallas kernels, shards(): pl.pallas_call(functools.partial(kernel, devices, layers, capacity), out_...  60.9 us
    unnamed x7, local copies, waits for them, and re-layouts  2.79 us

profile of v3, /device:TPU:0, one launch (start us, length us, event | category | flops | bytes accessed | tf_op | source)
XLA Modules:
  0.0 64.3 jit_solution(13306916218965875787)
XLA Ops:
  0.6 60.9 %shard_map.94 = (f32[16,16,128]{2,1,0:T(8,128)}, f32[16,16,128]{2,1,0:T(8,128)}, f32[3]{0:T(128)}) custom-call(bf16[16,128,128]{2,1,0:T(8,128)(2,1)} %wave_hbm.1, s32[16]{0:T(128)} %left_size_hbm.1, s32[64]{0:T(128)} %right_size_hbm.1, s32[64]{0:T(128)} %right_sector_hbm.1, bf16[2,16,128,128]{3,2,1,0:T(8,128)(2,1)} %left_hbm.1, ...), custom_call_target="tpu_custom_call" | custom-call | tf_op jit(solution)/shard_map/pallas_call | solution.py:494
  61.5 0.0 copy-start
  61.5 1.6 %copy.13 = f32[16,16,128]{2,1,0:T(8,128)} copy(f32[16,16,128]{2,1,0:T(8,128)} %get-tuple-element.6) | data formatting | bytes 262144
  63.1 0.0 copy-done
  63.1 0.0 copy-start.1
  63.1 0.7 %copy.14 = f32[16,16,128]{2,1,0:T(8,128)} copy(f32[16,16,128]{2,1,0:T(8,128)S(1)} %copy-done) | data formatting | bytes 262144
  63.8 0.0 copy-done.1
  63.8 0.5 copy.15
Async XLA Ops:
  61.5 1.6 %copy-start = (f32[16,16,128]{2,1,0:T(8,128)S(1)}, f32[16,16,128]{2,1,0:T(8,128)}, u32[]{:S(2)}) copy-start(f32[16,16,128]{2,1,0:T(8,128)} %get-tuple-element.7) | copy-start | bytes 393220
  63.1 0.7 %copy-start.1 = (f32[3]{0:T(128)S(1)}, f32[3]{0:T(128)}, u32[]{:S(2)}) copy-start(f32[3]{0:T(128)} %get-tuple-element.8) | copy-start | bytes 40
